TPU v7x, 512 devices: a whole 4x8x8 slice. The times are simulated.
512 devices in a mesh: node: 64 (over z, y_hi, core), local: 8 (over y_lo, x).
Axes of the slice: x: 4, y: 8 (y_hi: 4, y_lo: 2; y = y_hi * 2 + y_lo), z: 8, core: 2. Of those that a mesh axis runs over, the one named last changes fastest.
Arguments:
- tokens: bfloat16 [1536, 4096], P('node', 'local'), may hold values from -6 to 6
- cotangent: bfloat16 [1536, 4096], P('node', 'local'), may hold values from -0.75 to 0.75
- gate_weight: bfloat16 [14336, 4096], P('node', 'local'), may hold values from -0.09375 to 0.09375
- up_weight: bfloat16 [14336, 4096], P('node', 'local'), may hold values from -0.09375 to 0.09375
- down_weight: bfloat16 [14336, 4096], P('node', 'local'), may hold values from -0.046875 to 0.046875
- gate_moment: bfloat16 [14336, 4096], P('node', 'local'), may hold values from -6 to 6
- gate_square: bfloat16 [14336, 4096], P('node', 'local'), may hold values from 0.099609375 to 4
- up_moment: bfloat16 [14336, 4096], P('node', 'local'), may hold values from -6 to 6
- up_square: bfloat16 [14336, 4096], P('node', 'local'), may hold values from 0.099609375 to 4
- down_moment: bfloat16 [14336, 4096], P('node', 'local'), may hold values from -6 to 6
- down_square: bfloat16 [14336, 4096], P('node', 'local'), may hold values from 0.099609375 to 4
Outputs:
- input_grad: bfloat16 [1536, 4096], P('node', 'local')
- moment_gate: bfloat16 [14336, 4096], P('node', 'local')
- square_gate: bfloat16 [14336, 4096], P('node', 'local')
- update_gate: bfloat16 [14336, 4096], P('node', 'local')
- moment_up: bfloat16 [14336, 4096], P('node', 'local')
- square_up: bfloat16 [14336, 4096], P('node', 'local')
- update_up: bfloat16 [14336, 4096], P('node', 'local')
- moment_down: bfloat16 [14336, 4096], P('node', 'local')
- square_down: bfloat16 [14336, 4096], P('node', 'local')
- update_down: bfloat16 [14336, 4096], P('node', 'local')
All inputs are finite; a program needn't handle non-finite values.
Results may differ from a plain program's by a relative error of at most 0.0049.
Values may be sent and summed in bfloat16 or wider, within the bound.
A program may use at most 64 MiB of HBM per device.

v0:
```python
import jax
import jax.numpy as jnp
from jax import lax
from jax.sharding import PartitionSpec as P

ADAM_STEP = 20


beta_one = 0.9
beta_two = 0.95
epsilon = 1e-08


def activate(gate, up, back):
    sigma = jax.nn.sigmoid(gate)
    acted = gate * sigma
    hidden = (acted * up).astype(jnp.bfloat16)
    gate_grad = (back * up * sigma * (1.0 + gate * (1.0 - sigma))).astype(jnp.bfloat16)
    up_grad = (back * acted).astype(jnp.bfloat16)
    return (hidden, gate_grad, up_grad)


def adam_step(gradient, moment, square):
    moment_new = beta_one * moment.astype(jnp.float32) + (1.0 - beta_one) * gradient
    square_new = beta_two * square.astype(jnp.float32) + (1.0 - beta_two) * gradient * gradient
    scaled = moment_new / (1.0 - beta_one**ADAM_STEP)
    spread = jnp.sqrt(square_new / (1.0 - beta_two**ADAM_STEP)) + epsilon
    return (
        moment_new.astype(jnp.bfloat16),
        square_new.astype(jnp.bfloat16),
        (scaled / spread).astype(jnp.bfloat16),
    )


def per_device(
    tokens,
    cotangent,
    gate_weight,
    up_weight,
    down_weight,
    gate_moment,
    gate_square,
    up_moment,
    up_square,
    down_moment,
    down_square,
):
    features, upstream = (
        lax.all_gather(tokens, "node", axis=0, tiled=True),
        lax.all_gather(cotangent, "node", axis=0, tiled=True),
    )
    gate_part = jnp.einsum("td,fd->tf", features, gate_weight, preferred_element_type=jnp.float32)
    up_part = jnp.einsum("td,fd->tf", features, up_weight, preferred_element_type=jnp.float32)
    back_part = jnp.einsum("td,fd->tf", upstream, down_weight, preferred_element_type=jnp.float32)
    gate_full, up_full, back_full = lax.psum((gate_part, up_part, back_part), "local")
    hidden, gate_grad, up_grad = activate(gate_full, up_full, back_full)
    total = jnp.einsum("tf,fd->td", gate_grad, gate_weight, preferred_element_type=jnp.float32)
    input_grad = lax.psum_scatter(
        total + jnp.einsum("tf,fd->td", up_grad, up_weight, preferred_element_type=jnp.float32),
        "node",
        scatter_dimension=0,
        tiled=True,
    ).astype(jnp.bfloat16)
    grad_gate = jnp.einsum("tf,td->fd", gate_grad, features, preferred_element_type=jnp.float32)
    grad_up = jnp.einsum("tf,td->fd", up_grad, features, preferred_element_type=jnp.float32)
    grad_down = jnp.einsum("tf,td->fd", hidden, upstream, preferred_element_type=jnp.float32)
    moment_gate, square_gate, update_gate = adam_step(grad_gate, gate_moment, gate_square)
    moment_up, square_up, update_up = adam_step(grad_up, up_moment, up_square)
    moment_down, square_down, update_down = adam_step(grad_down, down_moment, down_square)
    return (
        input_grad,
        moment_gate,
        square_gate,
        update_gate,
        moment_up,
        square_up,
        update_up,
        moment_down,
        square_down,
        update_down,
    )


def solution(mesh):
    placed = (
        P("node", "local"),
        P("node", "local"),
        P("node", "local"),
        P("node", "local"),
        P("node", "local"),
        P("node", "local"),
        P("node", "local"),
        P("node", "local"),
        P("node", "local"),
        P("node", "local"),
        P("node", "local"),
    )
    return jax.shard_map(
        per_device,
        mesh=mesh,
        in_specs=placed,
        out_specs=(
            P("node", "local"),
            P("node", "local"),
            P("node", "local"),
            P("node", "local"),
            P("node", "local"),
            P("node", "local"),
            P("node", "local"),
            P("node", "local"),
            P("node", "local"),
            P("node", "local"),
        ),
        check_vma=False,
    )
```

profile of v0, /device:TPU:1, one launch (start us, length us, event | category | flops | bytes accessed | tf_op | source)
XLA Modules:
  0.0 461.6 jit_solution(8645759389895621162)
XLA Ops:
  7.2 0.0 copy-start
  7.2 0.0 all-gather.5.cloned.1.call-start
  7.2 0.7 all-gather.5.cloned.1.call-update
  7.9 0.0 all-gather.3.cloned.1.call-start
  8.0 0.7 all-gather.3.cloned.1.call-update
  8.7 0.0 copy-start.5
  8.7 0.0 all-reduce.3.cloned.1.call-start
  8.7 92.3 %all-gather.5.cloned.1.call-done = bf16[1536,512]{1,0:T(8,128)(2,1)} async-done(((bf16[24,512]{1,0:T(8,128)(2,1)}), bf16[1536,512]{1,0:T(8,128)(2,1)}) %all-gather.5.cloned.1.call-update) | async-done | bytes 1572880 | tf_op jit(solution)/shard_map/all_gather | solution.py:49
  101.0 0.0 copy-done
  101.0 0.0 copy-start.1
  101.0 3.3 fusion.15
  104.3 0.0 copy-done.5
  104.3 0.0 copy-done.1
  104.3 0.0 copy-start.6
  104.3 1.8 fusion.14
  106.1 78.1 %all-gather.3.cloned.1.call-done = bf16[1536,512]{1,0:T(8,128)(2,1)} async-done(((bf16[24,512]{1,0:T(8,128)(2,1)}), bf16[1536,512]{1,0:T(8,128)(2,1)}) %all-gather.3.cloned.1.call-update) | async-done | bytes 1572880 | tf_op jit(solution)/shard_map/all_gather | solution.py:50
  184.3 0.0 copy-done.6
  184.3 3.2 fusion.13
  187.5 0.0 all-reduce.3.cloned.1.call-update
  187.5 0.0 reduce-scatter.2.cloned.1.call-start
  187.6 111.3 %all-reduce.3.cloned.1.call-done = (f32[1536,224]{0,1:T(8,128)}, f32[1536,224]{0,1:T(8,128)}, f32[1536,224]{0,1:T(8,128)}) async-done(((f32[1536,224]{0,1:T(8,128)}, f32[1536,224]{0,1:T(8,128)}, f32[1536,224]{0,1:T(8,128)}), (f32[1536,224]{0,1:T(8,128)}, f32[1536,224]{0,1:T(8,128)}, f32[1536,224]{0,1:T(8,128)})) %all-reduce.3.cloned.1.call-update) | async-done | bytes 4128784 | tf_op jit(solution)/shard_map/psum | solution.py:55
  298.9 3.0 multiply_convert_fusion.1
  301.9 0.6 fusion.16
  302.5 2.3 convolution_add_fusion
  304.8 0.0 copy-start.7
  304.8 0.0 reduce-scatter.2.cloned.1.call-update
  304.8 0.9 copy-done.7
  305.7 0.0 copy-start.8
  305.7 0.0 copy-start.9
  305.7 2.6 divide_convert_fusion.1
  308.3 0.0 copy-done.8
  308.3 0.0 copy-done.9
  308.3 0.0 copy-start.2
  308.3 0.0 copy-start.3
  308.4 0.0 copy-start.4
  308.4 0.0 copy-start.10
  308.4 0.0 copy-start.11
  308.4 1.6 divide_convert_fusion.2
  310.0 0.0 copy-done.2
  310.0 0.2 copy-done.3
  310.2 0.6 copy-done.4
  310.8 0.0 copy-done.10
  310.8 0.1 copy-done.11
  310.9 1.7 divide_convert_fusion
  312.6 141.1 %reduce-scatter.2.cloned.1.call-done = f32[24,512]{1,0:T(8,128)} async-done(((f32[1536,512]{1,0:T(8,128)}), f32[24,512]{1,0:T(8,128)}) %reduce-scatter.2.cloned.1.call-update) | async-done | bytes 49168 | tf_op jit(solution)/shard_map/reduce_scatter | solution.py:58
  453.7 1.4 convert_element_type.59
Async XLA Ops:
  7.2 93.8 %copy-start = (bf16[224,512]{1,0:T(8,128)(2,1)S(1)}, bf16[224,512]{1,0:T(8,128)(2,1)}, u32[]{:S(2)}) copy-start(bf16[224,512]{1,0:T(8,128)(2,1)} %param.13) | copy-start | bytes 688132
  7.2 93.8 %all-gather.5.cloned.1.call-start = ((), (), s32[]{:S(2)}) async-start(), calls=%async_computation.2 | async-start | bytes 1597440 | tf_op jit(solution)/shard_map/all_gather | solution.py:49
  7.9 176.3 %all-gather.3.cloned.1.call-start = ((), (), s32[]{:S(2)}) async-start(), calls=%async_computation.1 | async-start | bytes 1597440 | tf_op jit(solution)/shard_map/all_gather | solution.py:50
  8.7 95.7 %copy-start.5 = (bf16[224,512]{1,0:T(8,128)(2,1)S(1)}, bf16[224,512]{1,0:T(8,128)(2,1)}, u32[]{:S(2)}) copy-start(bf16[224,512]{1,0:T(8,128)(2,1)} %param.14) | copy-start | bytes 688132
  8.7 290.2 %all-reduce.3.cloned.1.call-start = ((), (), s32[]{:S(2)}) async-start(), calls=%async_computation.4 | async-start | bytes 8257536 | tf_op jit(solution)/shard_map/psum | solution.py:55
  101.0 3.3 copy-start.1
  104.3 79.9 %copy-start.6 = (bf16[224,512]{1,0:T(8,128)(2,1)S(1)}, bf16[224,512]{1,0:T(8,128)(2,1)}, u32[]{:S(2)}) copy-start(bf16[224,512]{1,0:T(8,128)(2,1)} %param.15) | copy-start | bytes 688132
  187.5 266.1 %reduce-scatter.2.cloned.1.call-start = ((), (), s32[]{:S(2)}) async-start(), calls=%async_computation.3 | async-start | bytes 3194880 | tf_op jit(solution)/shard_map/reduce_scatter | solution.py:58
  304.8 0.9 copy-start.7
  305.7 2.6 copy-start.8
  305.7 2.6 copy-start.9
  308.3 1.7 copy-start.2
  308.3 1.9 copy-start.3
  308.4 2.5 copy-start.4
  308.4 2.5 copy-start.10
  308.4 2.5 copy-start.11
Sparse Core Ops, SparseCore 0:
  11.4 89.6 all-gather.4
  104.4 79.8 all-gather.2
  187.7 111.1 all-reduce.2
  304.9 148.7 reduce-scatter.1
where the time goes:
time: 465 us; the launch traced here: 462 us
  waiting for transfers between devices  424 us (91%)
  matrix products  17.1 us (4%)
  between operations  13.8 us (3%)
    reduce_scatter x1, waiting for transfers between devices, per_device(): lax.psum_scatter(total + jnp.einsum('tf,fd->td', up_grad, up_weight, pref...  141 us
    psum x1, waiting for transfers between devices, per_device(): lax.psum((gate_part, up_part, back_part), 'local')  111 us
    all_gather x1, waiting for transfers between devices, per_device(): lax.all_gather(tokens, 'node', axis=0, tiled=True)  92.3 us
    all_gather x1, waiting for transfers between devices, per_device(): lax.all_gather(cotangent, 'node', axis=0, tiled=True)  78.1 us
  transfers between devices with their start and end apart: 4, of which 4 were waited for; matrix products, arithmetic and copies ran while one was open for 2% of the time, Pallas kernels for 0%

commit v1 on v0

v1 whole, which is shorter than its diff:
```python
import functools

import jax
import jax.numpy as jnp
from jax import lax
from jax.experimental import pallas as pl
from jax.experimental.pallas import tpu as pltpu
from jax.sharding import PartitionSpec as P

ADAM_STEP = 20


beta_one = 0.9
beta_two = 0.95
epsilon = 1e-08

NZ, NYH, NC, NYL, NX = 8, 4, 2, 2, 4
MESH = pl.DeviceIdType.MESH
CHUNKS = ((0, 7), (1, 6), (2, 5), (3, 4))
PAD = 256


def adam_step(gradient, moment, square):
    moment_new = beta_one * moment.astype(jnp.float32) + (1.0 - beta_one) * gradient
    square_new = beta_two * square.astype(jnp.float32) + (1.0 - beta_two) * gradient * gradient
    scaled = moment_new / (1.0 - beta_one**ADAM_STEP)
    spread = jnp.sqrt(square_new / (1.0 - beta_two**ADAM_STEP)) + epsilon
    return (
        moment_new.astype(jnp.bfloat16),
        square_new.astype(jnp.bfloat16),
        (scaled / spread).astype(jnp.bfloat16),
    )


def nt(a, b):
    return lax.dot_general(a, b, (((1,), (1,)), ((), ())), preferred_element_type=jnp.float32)


def nn(a, b):
    return lax.dot_general(a, b, (((1,), (0,)), ((), ())), preferred_element_type=jnp.float32)


def tn(a, b):
    return lax.dot_general(a, b, (((0,), (0,)), ((), ())), preferred_element_type=jnp.float32)


def kernel(
    tok, cot, gw, uw, dw, ig, g_out,
    own_s, r_a, zb, wb, p_f, p_b, r_b, a_b, i_own, i_out, i_in, y_b, r_y, z_f, r_z, g_s, g_r,
    s_w, t_w, l_w, s_a, t_a, s_z, t_z, s_c, t_c, s_b, t_b, s_h, t_h, s_d, t_d, s_y, t_y, s_o, t_o, s_g, t_g,
):
    rows, feat = tok.shape
    units = gw.shape[0]
    block = NYH * rows
    chunk = 2 * block
    slice_ = chunk // NX
    node, local = lax.axis_index("node"), lax.axis_index("local")
    z, yh, c = node // (NYH * NC), (node // NC) % NYH, node % NC
    yl, x = local // NX, local % NX

    def at(dz=0, dyh=0, core=c, low=yl, dx=0):
        return (
            (((z + dz) % NZ) * NYH + (yh + dyh) % NYH) * NC + core,
            low * NX + (x + dx) % NX,
        )

    sibling, pair = at(core=1 - c), at(low=1 - yl)
    swapped = c != yl

    pending = []

    def send(src, dst, out, arrive, to):
        copy = pltpu.make_async_remote_copy(
            src_ref=src, dst_ref=dst, send_sem=out, recv_sem=arrive, device_id=to, device_id_type=MESH
        )
        copy.start()
        pending.append(copy)
        return copy

    own_w = []
    for p, ref in enumerate((gw, uw, dw)):
        copy = pltpu.make_async_copy(ref, wb.at[yl, p, pl.ds(0, units)], l_w.at[p])
        copy.start()
        own_w.append(copy)

    barrier = pltpu.get_barrier_semaphore()
    partners = [sibling, pair]
    partners += [at(dz=k) for k in range(1, NZ)]
    partners += [at(dx=k) for k in range(1, NX)]
    partners += [at(dyh=k, core=yl, low=c) for k in range(1, NYH)]
    for to in partners:
        pl.semaphore_signal(barrier, inc=1, device_id=to, device_id_type=MESH)

    @pl.when(swapped)
    def _():
        pl.semaphore_signal(barrier, inc=1, device_id=at(core=yl, low=c), device_id_type=MESH)

    own_s[...] = jnp.concatenate(
        [tok[...].astype(jnp.float32), cot[...].astype(jnp.float32)], axis=0
    ).astype(jnp.bfloat16)
    for h in range(2):
        for p in range(3):
            wb[h, p, units:PAD, :] = jnp.zeros((PAD - units, feat), jnp.bfloat16)
    pl.semaphore_wait(barrier, len(partners) + (c + yl) % 2)

    a_copies = []
    for k in range(1, NYH):
        a_copies.append(send(own_s, r_a.at[yh], s_a.at[k], t_a.at[k], at(dyh=k, core=yl, low=c)))
    here = pltpu.make_async_remote_copy(
        src_ref=own_s, dst_ref=r_a.at[yh], send_sem=s_a.at[0], recv_sem=t_a.at[0],
        device_id=at(core=yl, low=c), device_id_type=MESH,
    )

    @pl.when(swapped)
    def _():
        here.start()

    @pl.when(jnp.logical_not(swapped))
    def _():
        r_a[yh] = own_s[...]

    w_copies = []
    for p, ref in enumerate((gw, uw, dw)):
        w_copies.append(send(ref, wb.at[yl, p, pl.ds(0, units)], s_w.at[p], t_w.at[p], pair))

    for copy in a_copies:
        copy.wait_recv()

    @pl.when(swapped)
    def _():
        here.wait()

    for kind in range(2):
        zb[c, 0, kind] = jnp.concatenate(
            [r_a[j].astype(jnp.float32)[kind * rows : (kind + 1) * rows] for j in range(NYH)], axis=0
        ).astype(jnp.bfloat16)

    to_sibling = {}

    def share(slot, kind):
        to_sibling[slot, kind] = send(
            zb.at[c, slot, kind], zb.at[c, slot, kind], s_c.at[slot, kind], t_c.at[slot, kind], sibling
        )

    ring = {}

    def forward(step):
        for kind in range(2):
            if step < NZ // 2 or kind == 0:
                ring[0, step, kind] = send(
                    zb.at[c, (NZ - step + 1) % NZ, kind], zb.at[c, NZ - step, kind],
                    s_z.at[0, step - 1, kind], t_z.at[0, step - 1, kind], at(dz=1),
                )
            if step < NZ // 2 or kind == 1:
                ring[1, step, kind] = send(
                    zb.at[c, step - 1, kind], zb.at[c, step, kind],
                    s_z.at[1, step - 1, kind], t_z.at[1, step - 1, kind], at(dz=NZ - 1),
                )

    def ring_step(step):
        last = step == NZ // 2
        for kind in range(2):
            for way in range(2):
                if (way, step, kind) in ring:
                    ring[way, step, kind].wait_recv()
            if not last:
                nxt = step + 1
                if nxt < NZ // 2 or kind == 0:
                    ring[0, nxt, kind] = send(
                        zb.at[c, NZ - step, kind], zb.at[c, NZ - nxt, kind],
                        s_z.at[0, step, kind], t_z.at[0, step, kind], at(dz=1),
                    )
                if nxt < NZ // 2 or kind == 1:
                    ring[1, nxt, kind] = send(
                        zb.at[c, step, kind], zb.at[c, nxt, kind],
                        s_z.at[1, step, kind], t_z.at[1, step, kind], at(dz=NZ - 1),
                    )
                share(NZ - step, kind)
                share(step, kind)
            else:
                share(step, kind)

    def wide(h, k, kind):
        first, second = CHUNKS[k]
        return jnp.concatenate([zb[h, first, kind], zb[h, second, kind]], axis=0)

    b_copies, c_copies, d_copies, y_copies, o_copies = {}, {}, {}, {}, {}

    def products(k):
        for slot in CHUNKS[k]:
            for kind in range(2):
                to_sibling[slot, kind].wait_recv()
        gate_up = jnp.zeros((chunk, 2 * PAD), jnp.float32)
        back = jnp.zeros((chunk, PAD), jnp.float32)
        for h in range(2):
            gate_up += nt(wide(h, k, 0), wb[h, 0:2].reshape(2 * PAD, feat))
            back += nt(wide(h, k, 1), wb[h, 2])
        p_f[k, :, 0 : 2 * PAD] = gate_up
        p_f[k, :, 2 * PAD :] = back
        p_b[k, :, 0 : 2 * PAD] = gate_up.astype(jnp.bfloat16)
        p_b[k, :, 2 * PAD :] = back.astype(jnp.bfloat16)
        for d in range(1, NX):
            theirs = pl.multiple_of(((x + d) % NX) * slice_, slice_)
            b_copies[k, d] = send(
                p_b.at[k, pl.ds(theirs, slice_)], r_b.at[k, d - 1], s_b.at[k, d - 1], t_b.at[k, d - 1], at(dx=d)
            )

    def activate(k):
        for d in range(1, NX):
            b_copies[k, d].wait_recv()
        mine = pl.ds(pl.multiple_of(x * slice_, slice_), slice_)
        total = p_f[k, mine]
        for d in range(1, NX):
            total += r_b[k, d - 1].astype(jnp.float32)
        gate, up, back = total[:, :PAD], total[:, PAD : 2 * PAD], total[:, 2 * PAD :]
        sigma = jax.nn.sigmoid(gate)
        acted = gate * sigma
        a_b[k, mine, 0:PAD] = (back * up * sigma * (1.0 + gate * (1.0 - sigma))).astype(jnp.bfloat16)
        a_b[k, mine, PAD : 2 * PAD] = (back * acted).astype(jnp.bfloat16)
        a_b[k, mine, 2 * PAD :] = (acted * up).astype(jnp.bfloat16)
        for d in range(1, NX):
            c_copies[k, d] = send(
                a_b.at[k, mine], a_b.at[k, mine], s_h.at[k, d - 1], t_h.at[k, d - 1], at(dx=d)
            )

    def input_part(k):
        for d in range(1, NX):
            c_copies[k, d].wait_recv()
        grads = a_b[k, :, 0 : 2 * PAD]
        i_out[k] = nn(grads, wb[1 - c, 0:2].reshape(2 * PAD, feat))
        d_copies[k] = send(i_out.at[k], i_in.at[k], s_d.at[k], t_d.at[k], sibling)
        i_own[k] = nn(grads, wb[c, 0:2].reshape(2 * PAD, feat))

    def over_y(k):
        d_copies[k].wait_recv()
        total = i_own[k] + i_in[k]
        for j in range(NYH):
            y_b[k, j] = jnp.concatenate(
                [total[j * rows : (j + 1) * rows], total[block + j * rows : block + (j + 1) * rows]], axis=0
            ).astype(jnp.bfloat16)
        for d in range(1, NYH):
            y_copies[k, d] = send(
                y_b.at[k, (yh + d) % NYH], r_y.at[k, d], s_y.at[k, d], t_y.at[k, d], at(dyh=d, core=yl, low=c)
            )
        straight = pltpu.make_async_remote_copy(
            src_ref=y_b.at[k, yh], dst_ref=r_y.at[k, 0], send_sem=s_y.at[k, 0], recv_sem=t_y.at[k, 0],
            device_id=at(core=yl, low=c), device_id_type=MESH,
        )
        y_copies[k, 0] = straight

        @pl.when(swapped)
        def _():
            straight.start()

        @pl.when(jnp.logical_not(swapped))
        def _():
            r_y[k, 0] = y_b[k, yh]

    def over_z(k):
        for d in range(1, NYH):
            y_copies[k, d].wait_recv()

        @pl.when(swapped)
        def _():
            y_copies[k, 0].wait()

        total = r_y[k, 0].astype(jnp.float32)
        for d in range(1, NYH):
            total += r_y[k, d].astype(jnp.float32)
        for n, slot in enumerate(CHUNKS[k]):
            z_f[slot] = total[n * rows : (n + 1) * rows]
            if slot != 0:
                o_copies[slot] = send(
                    z_f.at[slot], r_z.at[slot - 1], s_o.at[slot - 1], t_o.at[slot - 1], at(dz=slot)
                )

    g_copies = []

    def tokens_of(h, kind):
        return jnp.concatenate([zb[h, slot, kind] for pair_ in CHUNKS for slot in pair_], axis=0)

    acts = (0, 1, 2)
    kinds = (0, 0, 1)

    def weight_parts_out():
        for p in acts:
            grads = a_b[:, :, p * PAD : (p + 1) * PAD].reshape(len(CHUNKS) * chunk, PAD)
            part = tn(grads, tokens_of(1 - yl, kinds[p]))
            g_s[p] = part[:units].astype(jnp.bfloat16)
            g_copies.append(send(g_s.at[p], g_r.at[p], s_g.at[p], t_g.at[p], pair))

    def weight_parts_own():
        for p in acts:
            grads = a_b[:, :, p * PAD : (p + 1) * PAD].reshape(len(CHUNKS) * chunk, PAD)
            g_out[p] = tn(grads, tokens_of(yl, kinds[p]))[:units]

    forward(1)
    for kind in range(2):
        share(0, kind)
    for copy in own_w:
        copy.wait()
    ring_step(1)
    for copy in w_copies:
        copy.wait_recv()
    products(0)
    ring_step(2)
    products(1)
    activate(0)
    ring_step(3)
    products(2)
    activate(1)
    input_part(0)
    ring_step(4)
    products(3)
    activate(2)
    input_part(1)
    over_y(0)
    activate(3)
    input_part(2)
    over_y(1)
    over_z(0)
    input_part(3)
    weight_parts_out()
    over_y(2)
    over_y(3)
    over_z(1)
    weight_parts_own()
    over_z(2)
    over_z(3)
    for slot in range(1, NZ):
        o_copies[slot].wait_recv()
    total = z_f[0]
    for slot in range(1, NZ):
        total += r_z[slot - 1]
    ig[...] = total.astype(jnp.bfloat16)
    for p in acts:
        g_copies[p].wait_recv()
        g_out[p] += g_r[p].astype(jnp.float32)
    for copy in pending:
        copy.wait_send()


def per_device(
    tokens,
    cotangent,
    gate_weight,
    up_weight,
    down_weight,
    gate_moment,
    gate_square,
    up_moment,
    up_square,
    down_moment,
    down_square,
):
    rows, feat = tokens.shape
    units = gate_weight.shape[0]
    block = NYH * rows
    chunk = 2 * block
    part = chunk // NX
    n = len(CHUNKS)
    bf, f32 = jnp.bfloat16, jnp.float32
    dma = pltpu.SemaphoreType.DMA
    vmem = pl.BlockSpec(memory_space=pltpu.VMEM)
    anywhere = pl.BlockSpec(memory_space=pl.ANY)
    sems = [(3,), (3,), (3,)]
    sems += [(NYH,)] * 2
    sems += [(2, NZ // 2, 2)] * 2
    sems += [(NZ, 2)] * 2
    sems += [(n, NX - 1)] * 4
    sems += [(n,)] * 2
    sems += [(n, NYH)] * 2
    sems += [(NZ - 1,)] * 2
    sems += [(3,)] * 2
    input_grad, grads = pl.pallas_call(
        kernel,
        name="ffn_step",
        out_shape=(
            jax.ShapeDtypeStruct((rows, feat), bf),
            jax.ShapeDtypeStruct((3, units, feat), f32),
        ),
        in_specs=[vmem, vmem, anywhere, anywhere, anywhere],
        out_specs=(vmem, vmem),
        scratch_shapes=[
            pltpu.VMEM((2 * rows, feat), bf),
            pltpu.VMEM((NYH, 2 * rows, feat), bf),
            pltpu.VMEM((2, NZ, 2, block, feat), bf),
            pltpu.VMEM((2, 3, PAD, feat), bf),
            pltpu.VMEM((n, chunk, 3 * PAD), f32),
            pltpu.VMEM((n, chunk, 3 * PAD), bf),
            pltpu.VMEM((n, NX - 1, part, 3 * PAD), bf),
            pltpu.VMEM((n, chunk, 3 * PAD), bf),
            pltpu.VMEM((n, chunk, feat), f32),
            pltpu.VMEM((n, chunk, feat), f32),
            pltpu.VMEM((n, chunk, feat), f32),
            pltpu.VMEM((n, NYH, 2 * rows, feat), bf),
            pltpu.VMEM((n, NYH, 2 * rows, feat), bf),
            pltpu.VMEM((NZ, rows, feat), f32),
            pltpu.VMEM((NZ - 1, rows, feat), f32),
            pltpu.VMEM((3, units, feat), bf),
            pltpu.VMEM((3, units, feat), bf),
        ]
        + [dma(shape) for shape in sems],
        compiler_params=pltpu.CompilerParams(
            collective_id=0, has_side_effects=True, vmem_limit_bytes=48 * 2**20
        ),
    )(tokens, cotangent, gate_weight, up_weight, down_weight)
    moment_gate, square_gate, update_gate = adam_step(grads[0], gate_moment, gate_square)
    moment_up, square_up, update_up = adam_step(grads[1], up_moment, up_square)
    moment_down, square_down, update_down = adam_step(grads[2], down_moment, down_square)
    return (
        input_grad,
        moment_gate,
        square_gate,
        update_gate,
        moment_up,
        square_up,
        update_up,
        moment_down,
        square_down,
        update_down,
    )


def solution(mesh):
    spec = P("node", "local")
    return jax.shard_map(
        per_device,
        mesh=mesh,
        in_specs=(spec,) * 11,
        out_specs=(spec,) * 10,
        check_vma=False,
    )
```

time: 465 us -> 110 us (0.24)
  the two profiles are of different devices: /device:TPU:1 before, /device:TPU:9 now
where the time goes in v1:
time: 110 us
  Pallas kernels  101 us (92%)
  local copies, waits for them, and re-layouts  4.89 us (4%)
  other arithmetic  3.61 us (3%)
    pallas_call x1, Pallas kernels, per_device(): pl.pallas_call(kernel, name='ffn_step', out_shape=(jax.ShapeDtypeStruct((...  101 us
    unnamed x11, local copies, waits for them, and re-layouts  4.89 us
    convert_element_type x1, other arithmetic, adam_step(): (scaled / spread).astype(jnp.bfloat16)  3.61 us

profile of v1, /device:TPU:9, one launch (start us, length us, event | category | flops | bytes accessed | tf_op | source)
XLA Modules:
  0.0 110.0 jit_solution(4138296380380184499)
XLA Ops:
  0.6 0.0 copy-start
  0.7 0.9 copy-done
  1.6 0.0 copy-start.1
  1.6 0.9 copy-done.1
  2.5 0.0 copy-start.2
  2.5 0.9 copy-done.2
  3.5 0.0 copy-start.3
  3.5 0.7 copy-done.3
  4.2 0.0 copy-start.4
  4.2 0.7 copy-done.4
  4.9 100.8 %ffn_step.1 = (bf16[24,512]{1,0:T(8,128)(2,1)S(1)}, f32[3,224,512]{2,1,0:T(8,128)S(1)}) custom-call(bf16[24,512]{1,0:T(8,128)(2,1)S(1)} %copy-done.3, bf16[24,512]{1,0:T(8,128)(2,1)S(1)} %copy-done.4, bf16[224,512]{1,0:T(8,128)(2,1)S(1)} %copy-done, bf16[224,512]{1,0:T(8,128)(2,1)S(1)} %copy-done.1, bf16[224,512]{1,0:T(8,128)(2,1)S(1)} %copy-done.2), custom_call_target="tpu_custom_call" | custom-call | tf_op jit(solution)/shard_map/ffn_step/pallas_call | solution.py:375
  105.7 3.6 %divide_convert_fusion = (bf16[224,512]{1,0:T(8,128)(2,1)}, bf16[224,512]{1,0:T(8,128)(2,1)}, bf16[224,512]{1,0:T(8,128)(2,1)}, bf16[224,512]{1,0:T(8,128)(2,1)}...) fusion(f32[3,224,512]{2,1,0:T(8,128)S(1)} %get-tuple-element.13, ...), kind=kLoop, calls=%fused_computation.12 | loop fusion | flops 5505024 | bytes 4816896 | tf_op jit(solution)/shard_map/convert_element_type | solution.py:31
  109.3 0.6 copy.22
Async XLA Ops:
  0.6 0.9 copy-start
  1.6 0.9 copy-start.1
  2.5 0.9 copy-start.2
  3.5 0.7 copy-start.3
  4.2 0.7 copy-start.4

commit v2 on v0

v2 whole, which is shorter than its diff:
```python
import functools

import jax
import jax.numpy as jnp
from jax import lax
from jax.experimental import pallas as pl
from jax.experimental.pallas import tpu as pltpu
from jax.sharding import PartitionSpec as P

ADAM_STEP = 20


beta_one = 0.9
beta_two = 0.95
epsilon = 1e-08

NZ, NYH, NC, NYL, NX = 8, 4, 2, 2, 4
MESH = pl.DeviceIdType.MESH
CHUNKS = ((0, 7), (1, 6), (2, 5), (3, 4))
UB = 128
STRIP = 16


def adam_step(gradient, moment, square):
    moment_new = beta_one * moment.astype(jnp.float32) + (1.0 - beta_one) * gradient
    square_new = beta_two * square.astype(jnp.float32) + (1.0 - beta_two) * gradient * gradient
    scaled = moment_new * (1.0 / (1.0 - beta_one**ADAM_STEP))
    spread = jnp.sqrt(square_new * (1.0 / (1.0 - beta_two**ADAM_STEP))) + epsilon
    return (
        moment_new.astype(jnp.bfloat16),
        square_new.astype(jnp.bfloat16),
        (scaled / spread).astype(jnp.bfloat16),
    )


def nt(a, b):
    return lax.dot_general(a, b, (((1,), (1,)), ((), ())), preferred_element_type=jnp.float32)


def nn(a, b):
    return lax.dot_general(a, b, (((1,), (0,)), ((), ())), preferred_element_type=jnp.float32)


def tn(a, b):
    return lax.dot_general(a, b, (((0,), (0,)), ((), ())), preferred_element_type=jnp.float32)


def kernel(
    tok, cot, gw, uw, dw, gm, gs, um, us, dm, ds, ig, steps,
    raw, own_s, r_a, zb, wb, p_f, p_b, r_b, a_b, i_own, i_out, i_in, z_b, r_z, y_f, r_y, g_o, g_s, g_r, mv, o_v,
    l_t, l_m, l_o, l_w, s_w, t_w, s_a, t_a, s_z, t_z, s_c, t_c, s_b, t_b, s_h, t_h, s_d, t_d, s_o, t_o, s_y, t_y, s_g, t_g,
):
    rows, feat = tok.shape
    units = gw.shape[0]
    block = NYH * rows
    chunk = 2 * block
    slice_ = chunk // NX
    n_chunks = len(CHUNKS)
    cuts = ((0, UB), (UB, units - UB))
    node, local = lax.axis_index("node"), lax.axis_index("local")
    z, yh, c = node // (NYH * NC), (node // NC) % NYH, node % NC
    yl, x = local // NX, local % NX

    def at(dz=0, dyh=0, core=c, low=yl, dx=0):
        return (
            (((z + dz) % NZ) * NYH + (yh + dyh) % NYH) * NC + core,
            low * NX + (x + dx) % NX,
        )

    sibling, pair = at(core=1 - c), at(low=1 - yl)
    swapped = c != yl

    def send(src, dst, out, arrive, to):
        copy = pltpu.make_async_remote_copy(
            src_ref=src, dst_ref=dst, send_sem=out, recv_sem=arrive, device_id=to, device_id_type=MESH
        )
        copy.start()
        return copy

    def bytes_of(ref, sem):
        pltpu.make_async_copy(ref, ref, sem).wait()

    for kind, ref in enumerate((tok, cot)):
        pltpu.make_async_copy(ref, raw.at[kind], l_t).start()

    barrier = pltpu.get_barrier_semaphore()
    partners = [sibling, pair] + [at(dz=k) for k in range(1, NZ)]
    partners += [at(dx=k) for k in range(1, NX)]
    partners += [at(dyh=k, core=yl, low=c) for k in range(1, NYH)]
    for to in partners:
        pl.semaphore_signal(barrier, inc=1, device_id=to, device_id_type=MESH)

    @pl.when(swapped)
    def _():
        pl.semaphore_signal(barrier, inc=1, device_id=at(core=yl, low=c), device_id_type=MESH)

    for f, (first, count) in enumerate(cuts):
        for p, ref in enumerate((gw, uw, dw)):
            pltpu.make_async_copy(
                ref.at[pl.ds(first, count)], wb.at[yl, f, p, pl.ds(0, count)], l_w
            ).start()
    for p, refs in enumerate(((gm, gs), (um, us), (dm, ds))):
        for j, ref in enumerate(refs):
            pltpu.make_async_copy(ref, mv.at[p, j], l_m).start()
    for h in range(2):
        for p in range(3):
            wb[h, 1, p, units - UB :, :] = jnp.zeros((2 * UB - units, feat), jnp.bfloat16)
    bytes_of(raw, l_t)
    own_s[...] = jnp.concatenate(
        [raw[kind].astype(jnp.float32) for kind in range(2)], axis=0
    ).astype(jnp.bfloat16)
    pl.semaphore_wait(barrier, len(partners) + (c + yl) % 2)

    for k in range(1, NYH):
        send(own_s, r_a.at[yh], s_a.at[1], t_a.at[1], at(dyh=k, core=yl, low=c))
    here = pltpu.make_async_remote_copy(
        src_ref=own_s, dst_ref=r_a.at[yh], send_sem=s_a.at[0], recv_sem=t_a.at[0],
        device_id=at(core=yl, low=c), device_id_type=MESH,
    )

    @pl.when(swapped)
    def _():
        here.start()

    @pl.when(jnp.logical_not(swapped))
    def _():
        r_a[yh] = own_s[...]

    def weights_out(f):
        first, count = cuts[f]
        for p, ref in enumerate((gw, uw, dw)):
            send(ref.at[pl.ds(first, count)], wb.at[yl, f, p, pl.ds(0, count)], s_w, t_w.at[f], pair)

    def weights_in(f):
        bytes_of(wb.at[1 - yl, f, :, pl.ds(0, cuts[f][1])], t_w.at[f])

    ring = {}
    chunk_of = {slot: k for k, slots in enumerate(CHUNKS) for slot in slots}

    def share(slot, kind):
        send(zb.at[c, slot, kind], zb.at[c, slot, kind], s_c, t_c.at[chunk_of[slot]], sibling)

    def forward(step, kind, way):
        if step > NZ // 2 or (step == NZ // 2 and kind != way):
            return
        src, dst = ((NZ - step + 1) % NZ, NZ - step) if way == 0 else (step - 1, step)
        ring[way, step, kind] = send(
            zb.at[c, src, kind], zb.at[c, dst, kind],
            s_z, t_z.at[way, step - 1, kind], at(dz=1 if way == 0 else NZ - 1),
        )

    def ring_step(step):
        for kind in range(2):
            for way in range(2):
                if (way, step, kind) in ring:
                    ring[way, step, kind].wait_recv()
                    forward(step + 1, kind, way)
                    share(NZ - step if way == 0 else step, kind)

    def tokens_in():
        bytes_of(r_a.at[pl.ds(0, NYH - 1)], t_a.at[1])

        @pl.when(swapped)
        def _():
            here.wait()

        for kind in range(2):
            zb[c, 0, kind] = jnp.concatenate(
                [r_a[j].astype(jnp.float32)[kind * rows : (kind + 1) * rows] for j in range(NYH)], axis=0
            ).astype(jnp.bfloat16)
            for way in range(2):
                forward(1, kind, way)
        for kind in range(2):
            share(0, kind)

    def wide(h, k, kind):
        first, second = CHUNKS[k]
        return jnp.concatenate([zb[h, first, kind], zb[h, second, kind]], axis=0)

    shared = set()

    def siblings_in(k):
        if k not in shared:
            shared.add(k)
            bytes_of(zb.at[1 - c, pl.ds(0, 2)], t_c.at[k])

    d_copies = {}

    def products(f, k):
        siblings_in(k)
        gate_up = nt(wide(0, k, 0), wb[0, f, 0:2].reshape(2 * UB, feat))
        gate_up += nt(wide(1, k, 0), wb[1, f, 0:2].reshape(2 * UB, feat))
        back = nt(wide(0, k, 1), wb[0, f, 2])
        back += nt(wide(1, k, 1), wb[1, f, 2])
        p_f[f, k, :, 0 : 2 * UB] = gate_up
        p_f[f, k, :, 2 * UB :] = back
        p_b[f, k, :, 0 : 2 * UB] = gate_up.astype(jnp.bfloat16)
        p_b[f, k, :, 2 * UB :] = back.astype(jnp.bfloat16)
        for d in range(1, NX):
            theirs = pl.multiple_of(((x + d) % NX) * slice_, slice_)
            send(p_b.at[f, k, pl.ds(theirs, slice_)], r_b.at[f, k, d - 1], s_b, t_b.at[f, k], at(dx=d))

    def activate(f, k):
        bytes_of(r_b.at[f, k], t_b.at[f, k])
        mine = pl.ds(pl.multiple_of(x * slice_, slice_), slice_)
        total = p_f[f, k, mine]
        for d in range(1, NX):
            total += r_b[f, k, d - 1].astype(jnp.float32)
        gate, up, back = total[:, :UB], total[:, UB : 2 * UB], total[:, 2 * UB :]
        sigma = jax.nn.sigmoid(gate)
        acted = gate * sigma
        a_b[f, k, mine, 0:UB] = (back * up * sigma * (1.0 + gate * (1.0 - sigma))).astype(jnp.bfloat16)
        a_b[f, k, mine, UB : 2 * UB] = (back * acted).astype(jnp.bfloat16)
        a_b[f, k, mine, 2 * UB :] = (acted * up).astype(jnp.bfloat16)
        for d in range(1, NX):
            send(a_b.at[f, k, mine], a_b.at[f, k, mine], s_h, t_h.at[f, k], at(dx=d))

    def gathered(f, k):
        bytes_of(r_b.at[f, k], t_h.at[f, k])

    def input_part(k):
        def half(h):
            total = nn(a_b[0, k, :, 0 : 2 * UB], wb[h, 0, 0:2].reshape(2 * UB, feat))
            return total + nn(a_b[1, k, :, 0 : 2 * UB], wb[h, 1, 0:2].reshape(2 * UB, feat))

        i_out[k] = half(1 - c)
        d_copies[k] = send(i_out.at[k], i_in.at[k], s_d, t_d.at[k], sibling)
        i_own[k] = half(c)

    def over_z(k):
        d_copies[k].wait_recv()
        for n, slot in enumerate(CHUNKS[k]):
            part = slice(n * block, (n + 1) * block)
            total = i_own[k, part] + i_in[k, part]
            if slot == 0:
                y_f[...] = total
            else:
                z_b[slot - 1] = total.astype(jnp.bfloat16)
                send(z_b.at[slot - 1], r_z.at[slot - 1], s_o, t_o, at(dz=slot))

    def over_y():
        bytes_of(r_z, t_o)
        total = y_f[...]
        for slot in range(1, NZ):
            total += r_z[slot - 1].astype(jnp.float32)
        y_f[...] = total

        def part(j):
            return pl.ds(pl.multiple_of(j * rows, 8), rows)

        for d in range(1, NYH):
            send(y_f.at[part((yh + d) % NYH)], r_y.at[d], s_y.at[1], t_y.at[1], at(dyh=d, core=yl, low=c))
        straight = pltpu.make_async_remote_copy(
            src_ref=y_f.at[part(yh)], dst_ref=r_y.at[0], send_sem=s_y.at[0], recv_sem=t_y.at[0],
            device_id=at(core=yl, low=c), device_id_type=MESH,
        )

        @pl.when(swapped)
        def _():
            straight.start()

        @pl.when(jnp.logical_not(swapped))
        def _():
            r_y[0] = y_f[part(yh)]

        return straight

    def input_out(straight):
        bytes_of(r_y.at[pl.ds(1, NYH - 1)], t_y.at[1])

        @pl.when(swapped)
        def _():
            straight.wait()

        total = r_y[0]
        for d in range(1, NYH):
            total += r_y[d]
        ig[...] = total.astype(jnp.bfloat16)

    def tokens_of(h, kind):
        return jnp.concatenate([zb[h, slot, kind] for pair_ in CHUNKS for slot in pair_], axis=0)

    def weight_parts(f, h):
        grads = a_b[f].reshape(n_chunks * chunk, 3 * UB)
        both = tn(grads[:, : 2 * UB], tokens_of(h, 0))
        return both[:UB], both[UB:], tn(grads[:, 2 * UB :], tokens_of(h, 1))

    def weights_grad_pair(f):
        for p, part in enumerate(weight_parts(f, 1 - yl)):
            g_s[f, p] = part.astype(jnp.bfloat16)

    def weights_grad_out(f):
        count = cuts[f][1]
        for p in range(3):
            send(g_s.at[f, p, pl.ds(0, count)], g_r.at[f, p, pl.ds(0, count)], s_g, t_g.at[f], pair)

    def weights_grad_own(f):
        for p, part in enumerate(weight_parts(f, yl)):
            g_o[f, p] = part

    def adam(f):
        first, count = cuts[f]
        bytes_of(g_r.at[f, :, pl.ds(0, count)], t_g.at[f])
        for p in range(3):

            @pl.loop(0, count // STRIP)
            def _(i):
                here_ = pl.ds(pl.multiple_of(i * STRIP, STRIP), STRIP)
                there = pl.ds(pl.multiple_of(first + i * STRIP, STRIP), STRIP)
                gradient = g_o[f, p, here_] + g_r[f, p, here_].astype(jnp.float32)
                for j, value in enumerate(adam_step(gradient, mv[p, 0, there], mv[p, 1, there])):
                    o_v[3 * p + j, there] = value

            for j in range(3):
                part = pl.ds(first, count)
                pltpu.make_async_copy(o_v.at[3 * p + j, part], steps.at[3 * p + j, part], l_o).start()

    def sent_early():
        bytes_of(r_a.at[pl.ds(0, NYH - 1)], s_a.at[1])
        bytes_of(mv.at[:, 0], s_w)
        bytes_of(zb.at[0, pl.ds(0, NZ - 1)], s_z)
        bytes_of(zb.at[0], s_c)
        bytes_of(r_b, s_b)
        bytes_of(r_b, s_h)
        bytes_of(i_out, s_d)

    weights_out(0)
    tokens_in()
    weights_out(1)
    bytes_of(mv.at[:, 0], l_w)
    ring_step(1)
    weights_in(0)
    products(0, 0)
    ring_step(2)
    products(0, 1)
    activate(0, 0)
    weights_in(1)
    products(1, 0)
    products(1, 1)
    ring_step(3)
    products(0, 2)
    products(1, 2)
    activate(0, 1)
    activate(1, 0)
    ring_step(4)
    products(0, 3)
    products(1, 3)
    activate(1, 1)
    activate(0, 2)
    activate(1, 2)
    gathered(0, 0)
    gathered(1, 0)
    input_part(0)
    activate(0, 3)
    over_z(0)
    activate(1, 3)
    gathered(0, 1)
    gathered(1, 1)
    input_part(1)
    over_z(1)
    gathered(0, 2)
    gathered(1, 2)
    input_part(2)
    gathered(0, 3)
    weights_grad_pair(0)
    weights_grad_out(0)
    over_z(2)
    gathered(1, 3)
    input_part(3)
    weights_grad_pair(1)
    over_z(3)
    weights_grad_out(1)
    weights_grad_own(0)
    weights_grad_own(1)
    bytes_of(mv, l_m)
    sent_early()
    adam(0)
    straight = over_y()
    adam(1)
    bytes_of(z_b, s_o)
    bytes_of(mv.at[:, 0], s_g)
    bytes_of(o_v, l_o)
    input_out(straight)
    bytes_of(r_y.at[pl.ds(1, NYH - 1)], s_y.at[1])


def settle(ig, steps, *outs_and_sems):
    outs, sems = outs_and_sems[:-1], outs_and_sems[-1]
    copies = [pltpu.make_async_copy(ig, outs[0], sems.at[0])]
    for j in range(len(outs) - 1):
        copies.append(pltpu.make_async_copy(steps.at[j], outs[j + 1], sems.at[j + 1]))
    for copy in copies:
        copy.start()
    for copy in copies:
        copy.wait()


def per_device(
    tokens,
    cotangent,
    gate_weight,
    up_weight,
    down_weight,
    gate_moment,
    gate_square,
    up_moment,
    up_square,
    down_moment,
    down_square,
):
    rows, feat = tokens.shape
    units = gate_weight.shape[0]
    block = NYH * rows
    chunk = 2 * block
    part = chunk // NX
    n = len(CHUNKS)
    bf, f32 = jnp.bfloat16, jnp.float32
    dma = pltpu.SemaphoreType.DMA
    vmem = pl.BlockSpec(memory_space=pltpu.VMEM)
    hbm = pl.BlockSpec(memory_space=pltpu.HBM)
    sems = [(), (), (), ()]
    sems += [(), (2,)]
    sems += [(2,), (2,)]
    sems += [(), (2, NZ // 2, 2)]
    sems += [(), (n,)]
    sems += [(), (2, n), (), (2, n)]
    sems += [(), (n,)]
    sems += [(), ()]
    sems += [(2,), (2,)]
    sems += [(), (2,)]
    input_grad, steps = pl.pallas_call(
        kernel,
        name="ffn_step",
        out_shape=(
            jax.ShapeDtypeStruct((rows, feat), bf),
            jax.ShapeDtypeStruct((9, units, feat), bf),
        ),
        in_specs=[hbm] * 11,
        out_specs=(vmem, hbm),
        scratch_shapes=[
            pltpu.VMEM((2, rows, feat), bf),
            pltpu.VMEM((2 * rows, feat), bf),
            pltpu.VMEM((NYH, 2 * rows, feat), bf),
            pltpu.VMEM((2, NZ, 2, block, feat), bf),
            pltpu.VMEM((2, 2, 3, UB, feat), bf),
            pltpu.VMEM((2, n, chunk, 3 * UB), f32),
            pltpu.VMEM((2, n, chunk, 3 * UB), bf),
            pltpu.VMEM((2, n, NX - 1, part, 3 * UB), bf),
            pltpu.VMEM((2, n, chunk, 3 * UB), bf),
            pltpu.VMEM((n, chunk, feat), f32),
            pltpu.VMEM((n, chunk, feat), f32),
            pltpu.VMEM((n, chunk, feat), f32),
            pltpu.VMEM((NZ - 1, block, feat), bf),
            pltpu.VMEM((NZ - 1, block, feat), bf),
            pltpu.VMEM((block, feat), f32),
            pltpu.VMEM((NYH, rows, feat), f32),
            pltpu.VMEM((2, 3, UB, feat), f32),
            pltpu.VMEM((2, 3, UB, feat), bf),
            pltpu.VMEM((2, 3, UB, feat), bf),
            pltpu.VMEM((3, 2, units, feat), bf),
            pltpu.VMEM((9, units, feat), bf),
        ]
        + [dma(shape) if shape else dma for shape in sems],
        compiler_params=pltpu.CompilerParams(
            collective_id=0, has_side_effects=True, vmem_limit_bytes=60 * 2**20
        ),
    )(
        tokens, cotangent, gate_weight, up_weight, down_weight,
        gate_moment, gate_square, up_moment, up_square, down_moment, down_square,
    )
    return tuple(
        pl.pallas_call(
            settle,
            name="settle",
            out_shape=(jax.ShapeDtypeStruct((rows, feat), bf),)
            + (jax.ShapeDtypeStruct((units, feat), bf),) * 9,
            in_specs=[vmem, vmem],
            out_specs=(hbm,) * 10,
            scratch_shapes=[dma((10,))],
        )(input_grad, steps)
    )


def solution(mesh):
    spec = P("node", "local")
    return jax.shard_map(
        per_device,
        mesh=mesh,
        in_specs=(spec,) * 11,
        out_specs=(spec,) * 10,
        check_vma=False,
    )
```

time: 465 us -> 89.1 us (0.19)
  waiting for transfers between devices: 424 us -> 0 us
  Pallas kernels: 0 us -> 88.3 us
  matrix products: 17.1 us -> 0 us
  between operations: 13.8 us -> 0.65 us
    all_gather x2 -> x0, waiting for transfers between devices: 170 us -> none  [the longest x1 92.3 us: per_device(): lax.all_gather(tokens, 'node', axis=0, tiled=True)]
    reduce_scatter x1 -> x0, waiting for transfers between devices: 141 us -> none  [per_device(): lax.psum_scatter(total + jnp.einsum('tf,fd->td', up_grad, up_weight, pref...]
    psum x1 -> x0, waiting for transfers between devices: 111 us -> none  [per_device(): lax.psum((gate_part, up_part, back_part), 'local')]
    pallas_call x0 -> x2, Pallas kernels: none -> 88.3 us  [the longest x1 85.3 us: per_device(): pl.pallas_call(kernel, name='ffn_step', out_shape=(jax.ShapeDtypeStruct((...]
    dot_general x8 -> x0, matrix products: 17.1 us -> none  [the longest x1 3.31 us: per_device(): jnp.einsum('td,fd->tf', features, gate_weight, preferred_element_type=jnp...]
  transfers between devices with their start and end apart: 4 -> 0, of which waited for: 4 -> 0; matrix products, arithmetic and copies ran while one was open for 2% -> 0% of each run, Pallas kernels for 0% -> 0%
where the time goes in v2:
time: 89.1 us; the launch traced here: 88.9 us
  Pallas kernels  88.3 us (99%)
    pallas_call x1, Pallas kernels, per_device(): pl.pallas_call(kernel, name='ffn_step', out_shape=(jax.ShapeDtypeStruct((...  85.3 us
    pallas_call x1, Pallas kernels, per_device(): pl.pallas_call(settle, name='settle', out_shape=(jax.ShapeDtypeStruct((ro...  2.99 us

profile of v2, /device:TPU:1, one launch (start us, length us, event | category | flops | bytes accessed | tf_op | source)
XLA Modules:
  0.0 88.9 jit_solution(2147877599061015359)
XLA Ops:
  0.6 85.3 %ffn_step.1 = (bf16[24,512]{1,0:T(8,128)(2,1)}, bf16[9,224,512]{2,1,0:T(8,128)(2,1)}) custom-call(bf16[24,512]{1,0:T(8,128)(2,1)} %tok.1, bf16[24,512]{1,0:T(8,128)(2,1)} %cot.1, bf16[224,512]{1,0:T(8,128)(2,1)} %gw.1, bf16[224,512]{1,0:T(8,128)(2,1)} %uw.1, bf16[224,512]{1,0:T(8,128)(2,1)} %dw.1, bf16[224,512]{1,0:T(8,128)(2,1)} %gm.1, ...), custom_call_target="tpu_custom_call" | custom-call | tf_op jit(solution)/shard_map/ffn_step/pallas_call | solution.py:431
  86.0 3.0 %settle.1 = (bf16[24,512]{1,0:T(8,128)(2,1)}, bf16[224,512]{1,0:T(8,128)(2,1)}, bf16[224,512]{1,0:T(8,128)(2,1)}, bf16[224,512]{1,0:T(8,128)(2,1)}, bf16[224,512...) custom-call(bf16[24,512]{1,0:T(8,128)(2,1)} %get-tuple-element.12.ig, ...), custom_call_target="tpu_custom_call" | custom-call | tf_op jit(solution)/shard_map/settle/pallas_call | solution.py:472

commit v3 on v2

--- a/solution.py
+++ b/solution.py
@@ -16,8 +16,8 @@
 
 NZ, NYH, NC, NYL, NX = 8, 4, 2, 2, 4
 MESH = pl.DeviceIdType.MESH
-CHUNKS = ((0, 7), (1, 6), (2, 5), (3, 4))
-UB = 128
+CHUNKS = ((1, 7), (2, 6), (3, 5), (0, 4))
+FIRST, UB = 96, 128
 STRIP = 16
 
 
@@ -47,7 +47,7 @@
 
 def kernel(
     tok, cot, gw, uw, dw, gm, gs, um, us, dm, ds, ig, steps,
-    raw, own_s, r_a, zb, wb, p_f, p_b, r_b, a_b, i_own, i_out, i_in, z_b, r_z, y_f, r_y, g_o, g_s, g_r, mv, o_v,
+    raw, own_s, r_a, zb, wb, p_f, p_b, r_b, a_b, i_own, i_out, i_in, z_b, r_z, y_f, y_h, r_y, g_o, g_s, g_r, mv, o_v,
     l_t, l_m, l_o, l_w, s_w, t_w, s_a, t_a, s_z, t_z, s_c, t_c, s_b, t_b, s_h, t_h, s_d, t_d, s_o, t_o, s_y, t_y, s_g, t_g,
 ):
     rows, feat = tok.shape
@@ -56,7 +56,7 @@
     chunk = 2 * block
     slice_ = chunk // NX
     n_chunks = len(CHUNKS)
-    cuts = ((0, UB), (UB, units - UB))
+    cuts = ((0, FIRST), (FIRST, units - FIRST))
     node, local = lax.axis_index("node"), lax.axis_index("local")
     z, yh, c = node // (NYH * NC), (node // NC) % NYH, node % NC
     yl, x = local // NX, local % NX
@@ -94,17 +94,6 @@
     def _():
         pl.semaphore_signal(barrier, inc=1, device_id=at(core=yl, low=c), device_id_type=MESH)
 
-    for f, (first, count) in enumerate(cuts):
-        for p, ref in enumerate((gw, uw, dw)):
-            pltpu.make_async_copy(
-                ref.at[pl.ds(first, count)], wb.at[yl, f, p, pl.ds(0, count)], l_w
-            ).start()
-    for p, refs in enumerate(((gm, gs), (um, us), (dm, ds))):
-        for j, ref in enumerate(refs):
-            pltpu.make_async_copy(ref, mv.at[p, j], l_m).start()
-    for h in range(2):
-        for p in range(3):
-            wb[h, 1, p, units - UB :, :] = jnp.zeros((2 * UB - units, feat), jnp.bfloat16)
     bytes_of(raw, l_t)
     own_s[...] = jnp.concatenate(
         [raw[kind].astype(jnp.float32) for kind in range(2)], axis=0
@@ -133,6 +122,21 @@
 
     def weights_in(f):
         bytes_of(wb.at[1 - yl, f, :, pl.ds(0, cuts[f][1])], t_w.at[f])
+
+    def own_in():
+        for f, (first, count) in enumerate(cuts):
+            for p, ref in enumerate((gw, uw, dw)):
+                pltpu.make_async_copy(
+                    ref.at[pl.ds(first, count)], wb.at[yl, f, p, pl.ds(0, count)], l_w
+                ).start()
+        for p, refs in enumerate(((gm, gs), (um, us), (dm, ds))):
+            for j, ref in enumerate(refs):
+                pltpu.make_async_copy(ref, mv.at[p, j], l_m).start()
+        for f, (_, count) in enumerate(cuts):
+            for h in range(2):
+                for p in range(3):
+                    if count < UB:
+                        wb[h, f, p, count:, :] = jnp.zeros((UB - count, feat), jnp.bfloat16)
 
     ring = {}
     chunk_of = {slot: k for k, slots in enumerate(CHUNKS) for slot in slots}
@@ -236,22 +240,30 @@
                 y_f[...] = total
             else:
                 z_b[slot - 1] = total.astype(jnp.bfloat16)
-                send(z_b.at[slot - 1], r_z.at[slot - 1], s_o, t_o, at(dz=slot))
-
-    def over_y():
-        bytes_of(r_z, t_o)
-        total = y_f[...]
+                for h in range(2):
+                    there = pl.ds(h * (feat // 2), feat // 2)
+                    send(
+                        z_b.at[slot - 1, :, there], r_z.at[slot - 1, :, there], s_o, t_o.at[h], at(dz=slot)
+                    )
+
+    def over_y(h):
+        there = pl.ds(h * (feat // 2), feat // 2)
+        bytes_of(r_z.at[:, :, there], t_o.at[h])
+        total = y_f[:, there]
         for slot in range(1, NZ):
-            total += r_z[slot - 1].astype(jnp.float32)
-        y_f[...] = total
+            total += r_z[slot - 1, :, there].astype(jnp.float32)
+        y_h[h] = total
 
         def part(j):
             return pl.ds(pl.multiple_of(j * rows, 8), rows)
 
         for d in range(1, NYH):
-            send(y_f.at[part((yh + d) % NYH)], r_y.at[d], s_y.at[1], t_y.at[1], at(dyh=d, core=yl, low=c))
+            send(
+                y_h.at[h, part((yh + d) % NYH)], r_y.at[h, d], s_y.at[h, 1], t_y.at[h, 1],
+                at(dyh=d, core=yl, low=c),
+            )
         straight = pltpu.make_async_remote_copy(
-            src_ref=y_f.at[part(yh)], dst_ref=r_y.at[0], send_sem=s_y.at[0], recv_sem=t_y.at[0],
+            src_ref=y_h.at[h, part(yh)], dst_ref=r_y.at[h, 0], send_sem=s_y.at[h, 0], recv_sem=t_y.at[h, 0],
             device_id=at(core=yl, low=c), device_id_type=MESH,
         )
 
@@ -261,21 +273,23 @@
 
         @pl.when(jnp.logical_not(swapped))
         def _():
-            r_y[0] = y_f[part(yh)]
+            r_y[h, 0] = y_h[h, part(yh)]
 
         return straight
 
-    def input_out(straight):
-        bytes_of(r_y.at[pl.ds(1, NYH - 1)], t_y.at[1])
+    def input_out(h, straight):
+        there = pl.ds(h * (feat // 2), feat // 2)
+        bytes_of(r_y.at[h, pl.ds(1, NYH - 1)], t_y.at[h, 1])
 
         @pl.when(swapped)
         def _():
             straight.wait()
 
-        total = r_y[0]
+        total = r_y[h, 0]
         for d in range(1, NYH):
-            total += r_y[d]
-        ig[...] = total.astype(jnp.bfloat16)
+            total += r_y[h, d]
+        ig[:, there] = total.astype(jnp.bfloat16)
+        bytes_of(r_y.at[h, pl.ds(1, NYH - 1)], s_y.at[h, 1])
 
     def tokens_of(h, kind):
         return jnp.concatenate([zb[h, slot, kind] for pair_ in CHUNKS for slot in pair_], axis=0)
@@ -325,6 +339,7 @@
         bytes_of(i_out, s_d)
 
     weights_out(0)
+    own_in()
     tokens_in()
     weights_out(1)
     bytes_of(mv.at[:, 0], l_w)
@@ -338,14 +353,14 @@
     products(1, 0)
     products(1, 1)
     ring_step(3)
+    activate(0, 1)
     products(0, 2)
     products(1, 2)
-    activate(0, 1)
     activate(1, 0)
     ring_step(4)
+    activate(1, 1)
     products(0, 3)
     products(1, 3)
-    activate(1, 1)
     activate(0, 2)
     activate(1, 2)
     gathered(0, 0)
@@ -375,24 +390,25 @@
     bytes_of(mv, l_m)
     sent_early()
     adam(0)
-    straight = over_y()
+    halves = [over_y(0), over_y(1)]
     adam(1)
     bytes_of(z_b, s_o)
     bytes_of(mv.at[:, 0], s_g)
     bytes_of(o_v, l_o)
-    input_out(straight)
-    bytes_of(r_y.at[pl.ds(1, NYH - 1)], s_y.at[1])
-
-
-def settle(ig, steps, *outs_and_sems):
-    outs, sems = outs_and_sems[:-1], outs_and_sems[-1]
-    copies = [pltpu.make_async_copy(ig, outs[0], sems.at[0])]
-    for j in range(len(outs) - 1):
-        copies.append(pltpu.make_async_copy(steps.at[j], outs[j + 1], sems.at[j + 1]))
-    for copy in copies:
-        copy.start()
-    for copy in copies:
-        copy.wait()
+    for h in range(2):
+        input_out(h, halves[h])
+
+
+def settle(ig, steps, *rest):
+    outs, (ig_v, steps_v, sem_in, sem_out) = rest[:10], rest[10:]
+    ways = [(ig, ig_v, outs[0])] + [(steps.at[j], steps_v.at[j], outs[j + 1]) for j in range(9)]
+    for n, (src, mid, _) in enumerate(ways):
+        pltpu.make_async_copy(src, mid, sem_in.at[n]).start()
+    for n, (src, mid, dst) in enumerate(ways):
+        pltpu.make_async_copy(src, mid, sem_in.at[n]).wait()
+        pltpu.make_async_copy(mid, dst, sem_out.at[n]).start()
+    for n, (_, mid, dst) in enumerate(ways):
+        pltpu.make_async_copy(mid, dst, sem_out.at[n]).wait()
 
 
 def per_device(
@@ -425,8 +441,8 @@
     sems += [(), (n,)]
     sems += [(), (2, n), (), (2, n)]
     sems += [(), (n,)]
-    sems += [(), ()]
-    sems += [(2,), (2,)]
+    sems += [(), (2,)]
+    sems += [(2, 2), (2, 2)]
     sems += [(), (2,)]
     input_grad, steps = pl.pallas_call(
         kernel,
@@ -453,7 +469,8 @@
             pltpu.VMEM((NZ - 1, block, feat), bf),
             pltpu.VMEM((NZ - 1, block, feat), bf),
             pltpu.VMEM((block, feat), f32),
-            pltpu.VMEM((NYH, rows, feat), f32),
+            pltpu.VMEM((2, block, feat // 2), f32),
+            pltpu.VMEM((2, NYH, rows, feat // 2), f32),
             pltpu.VMEM((2, 3, UB, feat), f32),
             pltpu.VMEM((2, 3, UB, feat), bf),
             pltpu.VMEM((2, 3, UB, feat), bf),
@@ -474,9 +491,11 @@
             name="settle",
             out_shape=(jax.ShapeDtypeStruct((rows, feat), bf),)
             + (jax.ShapeDtypeStruct((units, feat), bf),) * 9,
-            in_specs=[vmem, vmem],
+            in_specs=[hbm, hbm],
             out_specs=(hbm,) * 10,
-            scratch_shapes=[dma((10,))],
+            scratch_shapes=[
+                pltpu.VMEM((rows, feat), bf), pltpu.VMEM((9, units, feat), bf), dma((10,)), dma((10,)),
+            ],
         )(input_grad, steps)
     )
 

time: 89.1 us -> 85 us (0.954)
  Pallas kernels: 88.3 us -> 83.8 us
    pallas_call x1, Pallas kernels: 85.3 us -> 81.3 us  [per_device(): pl.pallas_call(kernel, name='ffn_step', out_shape=(jax.ShapeDtypeStruct((...]
where the time goes in v3:
time: 85 us; the launch traced here: 84.5 us
  Pallas kernels  83.8 us (99%)
    pallas_call x1, Pallas kernels, per_device(): pl.pallas_call(kernel, name='ffn_step', out_shape=(jax.ShapeDtypeStruct((...  81.3 us
    pallas_call x1, Pallas kernels, per_device(): pl.pallas_call(settle, name='settle', out_shape=(jax.ShapeDtypeStruct((ro...  2.53 us

profile of v3, /device:TPU:1, one launch (start us, length us, event | category | flops | bytes accessed | tf_op | source)
XLA Modules:
  0.0 84.5 jit_solution(12074013732980980435)
XLA Ops:
  0.6 81.3 %ffn_step.1 = (bf16[24,512]{1,0:T(8,128)(2,1)}, bf16[9,224,512]{2,1,0:T(8,128)(2,1)}) custom-call(bf16[24,512]{1,0:T(8,128)(2,1)} %tok.1, bf16[24,512]{1,0:T(8,128)(2,1)} %cot.1, bf16[224,512]{1,0:T(8,128)(2,1)} %gw.1, bf16[224,512]{1,0:T(8,128)(2,1)} %uw.1, bf16[224,512]{1,0:T(8,128)(2,1)} %dw.1, bf16[224,512]{1,0:T(8,128)(2,1)} %gm.1, ...), custom_call_target="tpu_custom_call" | custom-call | tf_op jit(solution)/shard_map/ffn_step/pallas_call | solution.py:447
  81.9 2.5 %settle.1 = (bf16[24,512]{1,0:T(8,128)(2,1)}, bf16[224,512]{1,0:T(8,128)(2,1)}, bf16[224,512]{1,0:T(8,128)(2,1)}, bf16[224,512]{1,0:T(8,128)(2,1)}, bf16[224,512...) custom-call(bf16[24,512]{1,0:T(8,128)(2,1)} %get-tuple-element.12.ig, ...), custom_call_target="tpu_custom_call" | custom-call | tf_op jit(solution)/shard_map/settle/pallas_call | solution.py:489
